TPU v7x, 256 devices: a whole 4x4x8 slice. The times are simulated.
256 devices in a mesh: sect: 4 (over z_hi), ctx: 8 (over z_lo, y), tp: 8 (over x, core).
Axes of the slice: x: 4, y: 4, z: 8 (z_hi: 4, z_lo: 2; z = z_hi * 2 + z_lo), core: 2. Of those that a mesh axis runs over, the one named last changes fastest.
Arguments:
- patches: bfloat16 [4096, 1280], P(('sect', 'ctx')), may hold values from -6 to 6
- patch_gain: float32 [1280], replicated, may hold values from 0.25 to 1.75
- patch_shift: float32 [1280], replicated, may hold values from -3 to 3
- encoder_up: bfloat16 [1280, 5120], P(None, 'tp'), may hold values from -0.15625 to 0.15625
- encoder_down: bfloat16 [5120, 1280], P('tp'), may hold values from -0.078125 to 0.078125
- proj_weight: bfloat16 [1280, 8192], P(None, 'tp'), may hold values from -0.15625 to 0.15625
- hidden_text: bfloat16 [8192, 8192], P(('sect', 'ctx'), 'tp'), may hold values from -180 to 180
- slot_source: int32 [64], P(('sect', 'ctx')), may hold values from 0 to 4, as said below
- norm_gain: float32 [8192], P('tp'), may hold values from 0.25 to 1.75
- kv_weight: bfloat16 [2048, 8192], P(None, 'tp'), may hold values from -0.0625 to 0.0625
- queries: bfloat16 [8192, 4096], P(('sect', 'ctx'), 'tp'), may hold values from -40 to 40
Outputs:
- attended: bfloat16 [8192, 4096], P(('sect', 'ctx'), 'tp')
Inputs may be any that keep to these rules, and one draw needn't show every extreme that they name: `slot_source`: for each ctx index, the slots of the blocks with that index carry each value 0 to 3 exactly once, all other slots 4.
All inputs are finite; a program needn't handle non-finite values.
Results may differ from a plain program's by a relative error of at most 0.019.
Values may be sent and summed in bfloat16 or wider, within the bound.
No kernel may reach another device: no remote copies, remote signals or barrier semaphores. Data moves between devices by JAX's collectives and lax.ppermute only.
A program may use at most 128 MiB of HBM per device.

v0:
```python
from functools import partial
import math
import jax
import jax.numpy as jnp
from jax import lax
from jax.sharding import PartitionSpec as P

D = 8192
HEAD = 128
Q_HEADS = 32
KV_HEADS = 8
PATCHES = 128


def layer_norm(values, norm_scale, norm_shift):
    widened = values.astype(jnp.float32)
    center = jnp.mean(widened, axis=-1, keepdims=True)
    spread = jnp.mean(jnp.square(widened - center), axis=-1, keepdims=True)
    return ((widened - center) * lax.rsqrt(spread + 1e-06) * norm_scale + norm_shift).astype(
        jnp.bfloat16
    )


def rotate_keys(keys_in, positions):
    half_size = keys_in.shape[-2] // 2
    frequencies = jnp.exp(
        jnp.arange(half_size, dtype=jnp.float32) * (-2.0 * math.log(500000.0) / (2 * half_size))
    )
    angles = positions[None, :] * frequencies[:, None]
    cosine_table = jnp.cos(angles)
    sine_table = jnp.sin(angles)
    first_half = keys_in[..., :half_size, :]
    second_half = keys_in[..., half_size:, :]
    return jnp.concatenate(
        [
            first_half * cosine_table - second_half * sine_table,
            second_half * cosine_table + first_half * sine_table,
        ],
        axis=-2,
    )


def attend_update(state_now, queries_blk, query_pos, keys_blk, values_blk, key_pos):
    running_max, running_sum, accumulated = state_now
    scale_value = queries_blk.shape[-1] ** (-0.5)
    scores = (
        jnp.einsum("rkgd,kdn->kgrn", queries_blk, keys_blk, preferred_element_type=jnp.float32)
        * scale_value
    )
    allowed = query_pos[:, None] >= key_pos[None, :]
    scores = jnp.where(allowed, scores, -jnp.inf)
    new_max = jnp.maximum(running_max, jnp.max(scores, axis=-1))
    weights = jnp.exp(scores - new_max[..., None])
    running_sum = jnp.sum(weights, axis=-1)
    mixed_rows = jnp.einsum(
        "kgrn,kdn->kgrd",
        weights.astype(jnp.bfloat16),
        values_blk,
        preferred_element_type=jnp.float32,
    )
    accumulated = mixed_rows
    return (new_max, running_sum, accumulated)


def keep_state(state_now):
    return state_now


def fold_step(states, fragment, first_index, groups):
    key_tile, value_tile = fragment
    key_pos = jnp.arange(key_tile.shape[2], dtype=jnp.int32)
    updated = []
    for group_entry, state_now in zip(groups, states):
        group_queries, group_first = group_entry
        row_count = group_queries.shape[0]
        query_pos = group_first + jnp.arange(row_count, dtype=jnp.int32)
        runner = partial(
            attend_update,
            queries_blk=group_queries,
            query_pos=query_pos,
            keys_blk=key_tile,
            values_blk=value_tile,
            key_pos=key_pos,
        )
        updated.append(
            lax.cond(first_index <= group_first + row_count - 1, runner, keep_state, state_now)
        )
    return tuple(updated)


def initial_state(kv_count, group_size, row_count):
    return (
        jnp.full((kv_count, group_size, row_count), -1e30, jnp.float32),
        jnp.zeros((kv_count, group_size, row_count), jnp.float32),
        jnp.zeros((kv_count, group_size, row_count, HEAD), jnp.float32),
    )


def finish_state(state_now):
    final_max, final_sum, final_acc = state_now
    result = final_acc / final_sum[..., None]
    return jnp.transpose(result, (2, 0, 1, 3)).reshape(result.shape[2], -1).astype(jnp.bfloat16)


def body(
    patches,
    patch_gain,
    patch_shift,
    encoder_up,
    encoder_down,
    proj_weight,
    hidden_text,
    slot_source,
    norm_gain,
    kv_weight,
    queries,
):
    normed_patches = layer_norm(patches, patch_gain, patch_shift)
    enc_hidden = jax.nn.gelu(
        jnp.dot(normed_patches, encoder_up, preferred_element_type=jnp.float32), approximate=False
    ).astype(jnp.bfloat16)
    partial_out = jnp.dot(enc_hidden, encoder_down, preferred_element_type=jnp.float32)
    summed_out = lax.psum(partial_out, "tp")
    encoded = (patches.astype(jnp.float32) + summed_out).astype(jnp.bfloat16)
    image_emb = jnp.dot(encoded, proj_weight, preferred_element_type=jnp.float32).astype(
        jnp.bfloat16
    )
    slot_total = slot_source.shape[0]
    slots_start = hidden_text.reshape(slot_total, PATCHES, hidden_text.shape[1])
    current = slots_start
    fragment = lax.all_gather(image_emb, "sect", axis=0, tiled=True)
    first_source = jnp.int32(0) // PATCHES
    for offset in range(fragment.shape[0] // PATCHES):
        chosen = (slot_source == first_source + offset)[:, None, None]
        current = jnp.where(
            chosen, fragment[offset * PATCHES : (offset + 1) * PATCHES][None], current
        )
    merged = current.reshape(hidden_text.shape)
    widened = merged.astype(jnp.float32)
    square_sums = lax.psum(jnp.sum(jnp.square(widened), axis=1), "tp")
    inverse = lax.rsqrt(square_sums / D + 1e-05)
    normed_hidden = (widened * inverse[:, None] * norm_gain[None, :]).astype(jnp.bfloat16)
    head_rows = kv_weight.shape[0] // lax.axis_size("tp")
    projected = lax.psum_scatter(
        lax.dot_general(
            kv_weight, normed_hidden, (((1,), (1,)), ((), ())), preferred_element_type=jnp.float32
        ),
        "tp",
        scatter_dimension=0,
        tiled=True,
    )
    row_total = queries.shape[0]
    kv_count = head_rows // (2 * HEAD)
    projected = projected.reshape(kv_count, 2, HEAD, row_total)
    block_number = lax.axis_index(("sect", "ctx"))
    first_position = block_number * row_total
    positions = (first_position + jnp.arange(row_total, dtype=jnp.int32)).astype(jnp.float32)
    rotated = rotate_keys(projected[:, 0], positions).astype(jnp.bfloat16)
    value_rows = projected[:, 1].astype(jnp.bfloat16)
    group_size = Q_HEADS // KV_HEADS
    grouped_queries = queries.reshape(row_total, kv_count, group_size, HEAD)
    groups = ((grouped_queries, first_position),)
    initial = tuple(
        [initial_state(kv_count, group_size, group_entry[0].shape[0]) for group_entry in groups]
    )
    folder = partial(fold_step, groups=groups)
    finals = folder(
        initial,
        (
            lax.all_gather(rotated, ("sect", "ctx"), axis=2, tiled=True),
            lax.all_gather(value_rows, ("sect", "ctx"), axis=2, tiled=True),
        ),
        jnp.int32(0),
    )
    results = [finish_state(state_now) for state_now in finals]
    return results[0]


def solution(mesh):
    in_specs = (
        P(("sect", "ctx"), None),
        P(),
        P(),
        P(None, "tp"),
        P("tp", None),
        P(None, "tp"),
        P(("sect", "ctx"), "tp"),
        P(("sect", "ctx")),
        P("tp"),
        P(None, "tp"),
        P(("sect", "ctx"), "tp"),
    )
    out_specs = P(("sect", "ctx"), "tp")
    return jax.shard_map(body, mesh=mesh, in_specs=in_specs, out_specs=out_specs, check_vma=False)
```

profile of v0, /device:TPU:8, one launch (start us, length us, event | category | flops | bytes accessed | tf_op | source)
XLA Modules:
  0.0 383.6 jit_solution(16793101043001423742)
XLA Ops:
  6.5 1.2 convert_reduce_fusion
  7.8 1.2 fusion.24
  9.0 4.4 %fusion.55 = f32[128,1280]{1,0:T(8,128)} fusion(bf16[640,1280]{1,0:T(8,128)(2,1)} %param.17, bf16[1280,640]{1,0:T(8,128)(2,1)} %param.16, bf16[128,1280]{1,0:T(8,128)(2,1)} %param.13, f32[1280]{0:T(1024)} %param.15, f32[1280]{0:T(1024)} %param.14, f32[128]{0:T(128)S(1)} %add_rsqrt_fusion.1, f32[128]{0:T(128)S(1)} %broadcast_multiply_fusion), kind=kOutput, calls=%fused_computation.67 | convolution fusion | flops 425738240 | bytes 4271104 | tf_op jit(solution)/shard_map/dot_general | solution.py:122
  13.4 0.0 all-reduce.2.cloned.1.call-update
  13.5 0.0 all-gather.5.cloned.1.call-start
  13.5 69.3 %all-reduce.2.cloned.1.call-done = f32[128,1280]{1,0:T(8,128)} async-done(((f32[128,1280]{1,0:T(8,128)}), f32[128,1280]{1,0:T(8,128)}) %all-reduce.2.cloned.1.call-update) | async-done | bytes 655376 | tf_op jit(solution)/shard_map/psum | solution.py:123
  82.9 2.3 convolution_convert_fusion
  85.2 0.0 reduce-scatter.2.cloned.1.call-start
  85.3 0.1 broadcast_bitcast_fusion.2
  85.3 0.1 broadcast_bitcast_fusion
  85.4 34.6 %all-gather.5.cloned.1.call-done = bf16[512,1024]{1,0:T(8,128)(2,1)} async-done(((bf16[128,1024]{1,0:T(8,128)(2,1)}), bf16[512,1024]{1,0:T(8,128)(2,1)}) %all-gather.5.cloned.1.call-update) | async-done | bytes 1048592 | tf_op jit(solution)/shard_map/all_gather | solution.py:131
  120.0 1.3 fusion.127
  121.3 1.6 fusion.19
  122.8 14.3 %psum.15 = f32[256]{0:T(256)S(1)} all-reduce(f32[256]{0:T(256)S(1)} %get-tuple-element.38), channel_id=1, replica_groups=mesh['sect'=4,'ctx'=8,'tp'=8] {'tp'}, use_global_device_ids=true, to_apply=%region_4.5 | all-reduce | flops 256 | bytes 2048 | tf_op jit(solution)/shard_map/psum | solution.py:140
  137.2 5.1 %convolution_bitcast_fusion = f32[2048,256]{0,1:T(8,128)} fusion(bf16[2048,1024]{1,0:T(8,128)(2,1)} %param.22, bf16[256,1024]{1,0:T(8,128)(2,1)} %get-tuple-element.39, f32[1024]{0:T(1024)S(1)} %copy-done.6, f32[256]{0:T(256)S(1)} %add_rsqrt_fusion), kind=kOutput, calls=%fused_computation.19 | convolution fusion | flops 1074790400 | bytes 6820864 | tf_op jit(solution)/shard_map/dot_general | solution.py:145
  142.3 0.0 all-gather.7.cloned.1.call-start
  142.4 31.3 %reduce-scatter.2.cloned.1.call-done = f32[256,256]{0,1:T(8,128)} async-done(((f32[2048,256]{0,1:T(8,128)}), f32[256,256]{0,1:T(8,128)}) %reduce-scatter.2.cloned.1.call-update) | async-done | bytes 262160 | tf_op jit(solution)/shard_map/reduce_scatter | solution.py:144
  173.7 1.1 copy.20
  174.8 0.3 fusion.93
  175.1 0.6 pad_maximum_fusion
  175.8 0.2 all-gather.9.cloned.1.call-start
  176.0 0.6 slice.47
  176.6 73.0 %all-gather.7.cloned.1.call-done = bf16[1,128,8192]{2,1,0:T(8,128)(2,1)} async-done(((bf16[1,128,256]{2,1,0:T(8,128)(2,1)}), bf16[1,128,8192]{2,1,0:T(8,128)(2,1)}) %all-gather.7.cloned.1.call-update) | async-done | bytes 2097168 | tf_op jit(solution)/shard_map/all_gather | solution.py:170
  249.6 76.4 %all-gather.9.cloned.1.call-done = bf16[1,1,128,8192]{3,2,1,0:T(8,128)(2,1)} async-done(((bf16[1,1,128,256]{3,2,1,0:T(8,128)(2,1)}), bf16[1,1,128,8192]{3,2,1,0:T(8,128)(2,1)}) %all-gather.9.cloned.1.call-update) | async-done | bytes 2097168 | tf_op jit(solution)/shard_map/all_gather | solution.py:171
  326.1 49.8 %conditional.1 = (f32[1,4,256]{2,1,0:T(4,128)S(1)}, f32[1,4,256,128]{3,2,1,0:T(8,128)S(1)}) conditional(s32[]{:T(128)} %convert_element_type.65, () %tuple.13, (s32[]{:T(128)}, s32[256]{0:T(256)S(1)}, s32[8192]{0:T(1024)S(1)}, bf16[1,128,8192]{2,1,0:T(8,128)(2,1)}, bf16[256,512]{1,0:T(8,128)(2,1)S(1)}, ...), branch_computations={%region_6.7_spmd, %region_7.10_spmd} | conditional | flops 4389338112 | bytes 122481712 | solution.py:86
  326.1 3.7 broadcast_compare_fusion
  329.8 15.6 %fusion.2 = (f32[4,256]{1,0:T(4,128)S(1)}, f32[8192,256,4]{1,0,2:T(8,128)}) fusion(pred[256,8192]{0,1:T(8,128)(4,1)S(1)} %broadcast_compare_fusion, bf16[1,128,8192]{2,1,0:T(8,128)(2,1)} %get-tuple-element.35, bf16[256,512]{1,0:T(8,128)(2,1)S(1)} %get-tuple-element.31), kind=kOutput, calls=%fused_computation.4 | convolution fusion | flops 2172648448 | bytes 38014976 | tf_op jit(solution)/shard_map/cond/branch_1_fun/rkgd,kdn->kgrn/dot_general | solution.py:47
  345.5 15.8 %fusion.10 = f32[1,4,256,128]{3,2,1,0:T(8,128)S(1)} fusion(bf16[1,128,8192]{2,1,0:T(8,128)(2,1)} %get-tuple-element.25, f32[8192,256,4]{1,0,2:T(8,128)} %get-tuple-element.41, f32[4,256]{1,0:T(4,128)S(1)} %broadcast_maximum_fusion, pred[256,8192]{0,1:T(8,128)(4,1)} %copy-done.1), kind=kOutput, calls=%fused_computation.12 | convolution fusion | flops 2181038080 | bytes 38277120 | tf_op jit(solution)/shard_map/cond/branch_1_fun/kgrn,kdn->kgrd/dot_general | solution.py:55
  361.2 14.6 %fusion.1 = f32[4,256]{1,0:T(4,128)S(1)} fusion(f32[8192,256,4]{1,0,2:T(8,128)} %get-tuple-element.41, f32[4,256]{1,0:T(4,128)S(1)} %broadcast_maximum_fusion, pred[256,8192]{0,1:T(8,128)(4,1)} %copy-done.1), kind=kLoop, calls=%fused_computation.3 | loop fusion | flops 33553408 | bytes 35659776 | tf_op jit(solution)/shard_map/cond/branch_1_fun/reduce_sum | solution.py:54
  375.9 0.2 fusion.57
  376.1 0.2 copy.22
  376.3 0.7 copy.33
  (30 shorter events, 0.2 us)
Async XLA Ops:
  6.5 76.3 %copy-start = (bf16[1280,1024]{1,0:T(8,128)(2,1)S(1)}, bf16[1280,1024]{1,0:T(8,128)(2,1)}, u32[]{:S(2)}) copy-start(bf16[1280,1024]{1,0:T(8,128)(2,1)} %param.18) | copy-start | bytes 7864324
  6.5 76.3 %all-reduce.2.cloned.1.call-start = ((), (), s32[]{:S(2)}) async-start(), calls=%async_computation.1 | async-start | bytes 1310720 | tf_op jit(solution)/shard_map/psum | solution.py:123
  9.0 73.8 %copy-start.2 = (bf16[128,1280]{1,0:T(8,128)(2,1)S(1)}, bf16[128,1280]{1,0:T(8,128)(2,1)}, u32[]{:S(2)}) copy-start(bf16[128,1280]{1,0:T(8,128)(2,1)} %param.13) | copy-start | bytes 983044
  13.4 71.8 %copy-start.4 = (s32[2]{0:T(128)S(1)}, s32[2]{0:T(128)}, u32[]{:S(2)}) copy-start(s32[2]{0:T(128)} %param.20) | copy-start | bytes 28
  13.4 107.8 %copy-start.3 = (bf16[256,1024]{1,0:T(8,128)(2,1)S(1)}, bf16[256,1024]{1,0:T(8,128)(2,1)}, u32[]{:S(2)}) copy-start(bf16[256,1024]{1,0:T(8,128)(2,1)} %param.19) | copy-start | bytes 1572868
  13.5 123.7 %copy-start.6 = (f32[1024]{0:T(1024)S(1)}, f32[1024]{0:T(1024)}, u32[]{:S(2)}) copy-start(f32[1024]{0:T(1024)} %param.21) | copy-start | bytes 12292
  13.5 106.5 %all-gather.5.cloned.1.call-start = ((), (), s32[]{:S(2)}) async-start(), calls=%async_computation.2 | async-start | bytes 1310720 | tf_op jit(solution)/shard_map/all_gather | solution.py:131
  85.2 88.5 %reduce-scatter.2.cloned.1.call-start = ((), (), s32[]{:S(2)}) async-start(), calls=%async_computation.3 | async-start | bytes 2359296 | tf_op jit(solution)/shard_map/reduce_scatter | solution.py:144
  137.2 188.9 %copy-start.5 = (bf16[256,512]{1,0:T(8,128)(2,1)S(1)}, bf16[256,512]{1,0:T(8,128)(2,1)}, u32[]{:S(2)}) copy-start(bf16[256,512]{1,0:T(8,128)(2,1)} %param.23) | copy-start | bytes 786436
  142.3 107.3 %all-gather.7.cloned.1.call-start = ((), (), s32[]{:S(2)}) async-start(), calls=%async_computation.4 | async-start | bytes 2162688 | tf_op jit(solution)/shard_map/all_gather | solution.py:170
  175.8 150.3 %all-gather.9.cloned.1.call-start = ((), (), s32[]{:S(2)}) async-start(), calls=%async_computation.5 | async-start | bytes 2162688 | tf_op jit(solution)/shard_map/all_gather | solution.py:171
  329.8 15.6 %copy-start.1 = (pred[256,8192]{0,1:T(8,128)(4,1)}, pred[256,8192]{0,1:T(8,128)(4,1)S(1)}, u32[]{:S(2)}) copy-start(pred[256,8192]{0,1:T(8,128)(4,1)S(1)} %broadcast_compare_fusion) | copy-start | bytes 6291460 | tf_op jit(solution)/shard_map/cond
Sparse Core Ops, SparseCore 0:
  13.6 69.2 all-reduce.1
  85.3 34.6 all-gather.4
  142.4 31.1 reduce-scatter.1
  176.0 73.6 all-gather.6
  252.0 74.0 all-gather.8
where the time goes:
time: 384 us
  waiting for transfers between devices  285 us (74%)
  matrix products  43.2 us (11%)
  other arithmetic  23.6 us (6%)
  blocking collectives  14.3 us (4%)
  between operations  13.3 us (3%)
  local copies, waits for them, and re-layouts  4.12 us (1%)
    all_gather x1, waiting for transfers between devices, body(): lax.all_gather(value_rows, ('sect', 'ctx'), axis=2, tiled=True)  76.4 us
    all_gather x1, waiting for transfers between devices, body(): lax.all_gather(rotated, ('sect', 'ctx'), axis=2, tiled=True)  73 us
    psum x1, waiting for transfers between devices, body(): summed_out = lax.psum(partial_out, 'tp')  69.3 us
    all_gather x1, waiting for transfers between devices, body(): fragment = lax.all_gather(image_emb, 'sect', axis=0, tiled=True)  34.6 us
    reduce_scatter x1, waiting for transfers between devices, body(): lax.psum_scatter(lax.dot_general(kv_weight, normed_hidden, (((1,), (1,)),...  31.3 us
    dot_general x1, matrix products, attend_update(): jnp.einsum('kgrn,kdn->kgrd', weights.astype(jnp.bfloat16), values_blk, pr...  15.8 us
    dot_general x1, matrix products, attend_update(): jnp.einsum('rkgd,kdn->kgrn', queries_blk, keys_blk, preferred_element_typ...  15.6 us
    reduce_sum x1, other arithmetic, attend_update(): running_sum = jnp.sum(weights, axis=-1)  14.6 us
  transfers between devices with their start and end apart: 5, of which 5 were waited for; matrix products, arithmetic and copies ran while one was open for 0% of the time, Pallas kernels for 0%

commit v1 on v0

--- a/solution.py
+++ b/solution.py
@@ -167,7 +167,12 @@
     finals = folder(
         initial,
         (
-            lax.all_gather(rotated, ("sect", "ctx"), axis=2, tiled=True),
+            jnp.concatenate(
+                lax.all_to_all(
+                    jnp.stack([rotated] * lax.axis_size(("sect", "ctx"))), ("sect", "ctx"), 0, 0
+                ),
+                axis=2,
+            ),
             lax.all_gather(value_rows, ("sect", "ctx"), axis=2, tiled=True),
         ),
         jnp.int32(0),

time: 384 us -> 325 us (0.85)
  waiting for transfers between devices: 285 us -> 214 us
  starting transfers between devices: 0.35 us -> 10.3 us
    all_gather x1 -> x0, waiting for transfers between devices: 73 us -> none  [body(): lax.all_gather(rotated, ('sect', 'ctx'), axis=2, tiled=True)]
    all_to_all x0 -> x1, starting transfers between devices: none -> 10.1 us  [body(): lax.all_to_all(jnp.stack([rotated] * lax.axis_size(('sect', 'ctx'))), ('s...]
  transfers between devices with their start and end apart: 5 -> 5, of which waited for: 5 -> 4; matrix products, arithmetic and copies ran while one was open for 0% -> 1% of each run, Pallas kernels for 0% -> 0%
where the time goes in v1:
time: 325 us
  waiting for transfers between devices  214 us (66%)
  matrix products  43.1 us (13%)
  other arithmetic  23.3 us (7%)
  blocking collectives  14.3 us (4%)
  between operations  13.3 us (4%)
  starting transfers between devices  10.3 us (3%)
  local copies, waits for them, and re-layouts  6.3 us (2%)
    all_gather x1, waiting for transfers between devices, body(): lax.all_gather(value_rows, ('sect', 'ctx'), axis=2, tiled=True)  79.1 us
    psum x1, waiting for transfers between devices, body(): summed_out = lax.psum(partial_out, 'tp')  69.3 us
    all_gather x1, waiting for transfers between devices, body(): fragment = lax.all_gather(image_emb, 'sect', axis=0, tiled=True)  34.6 us
    reduce_scatter x1, waiting for transfers between devices, body(): lax.psum_scatter(lax.dot_general(kv_weight, normed_hidden, (((1,), (1,)),...  31.3 us
    dot_general x1, matrix products, attend_update(): jnp.einsum('kgrn,kdn->kgrd', weights.astype(jnp.bfloat16), values_blk, pr...  15.8 us
    dot_general x1, matrix products, attend_update(): jnp.einsum('rkgd,kdn->kgrn', queries_blk, keys_blk, preferred_element_typ...  15.6 us
    reduce_sum x1, other arithmetic, attend_update(): running_sum = jnp.sum(weights, axis=-1)  14.6 us
    psum x1, blocking collectives, body(): square_sums = lax.psum(jnp.sum(jnp.square(widened), axis=1), 'tp')  14.3 us
  transfers between devices with their start and end apart: 5, of which 4 were waited for; matrix products, arithmetic and copies ran while one was open for 1% of the time, Pallas kernels for 0%

profile of v1, /device:TPU:8, one launch (start us, length us, event | category | flops | bytes accessed | tf_op | source)
XLA Modules:
  0.0 325.0 jit_solution(3339055922543097875)
XLA Ops:
  6.5 1.2 convert_reduce_fusion
  7.8 1.2 fusion.23
  9.0 4.4 %fusion.54 = f32[128,1280]{1,0:T(8,128)} fusion(bf16[640,1280]{1,0:T(8,128)(2,1)} %param.17, bf16[1280,640]{1,0:T(8,128)(2,1)} %param.16, bf16[128,1280]{1,0:T(8,128)(2,1)} %param.13, f32[1280]{0:T(1024)} %param.15, f32[1280]{0:T(1024)} %param.14, f32[128]{0:T(128)S(1)} %add_rsqrt_fusion.1, f32[128]{0:T(128)S(1)} %broadcast_multiply_fusion), kind=kOutput, calls=%fused_computation.66 | convolution fusion | flops 425738240 | bytes 4271104 | tf_op jit(solution)/shard_map/dot_general | solution.py:122
  13.5 0.0 all-gather.4.cloned.1.call-start
  13.5 69.3 %all-reduce.2.cloned.1.call-done = f32[128,1280]{1,0:T(8,128)} async-done(((f32[128,1280]{1,0:T(8,128)}), f32[128,1280]{1,0:T(8,128)}) %all-reduce.2.cloned.1.call-update) | async-done | bytes 655376 | tf_op jit(solution)/shard_map/psum | solution.py:123
  82.9 2.3 convolution_convert_fusion
  85.2 0.0 reduce-scatter.2.cloned.1.call-start
  85.3 0.1 broadcast_bitcast_fusion.2
  85.3 0.1 broadcast_bitcast_fusion
  85.4 34.6 %all-gather.4.cloned.1.call-done = bf16[512,1024]{1,0:T(8,128)(2,1)} async-done(((bf16[128,1024]{1,0:T(8,128)(2,1)}), bf16[512,1024]{1,0:T(8,128)(2,1)}) %all-gather.4.cloned.1.call-update) | async-done | bytes 1048592 | tf_op jit(solution)/shard_map/all_gather | solution.py:131
  120.0 1.3 fusion.128
  121.3 1.6 fusion.18
  122.9 14.3 %psum.15 = f32[256]{0:T(256)S(1)} all-reduce(f32[256]{0:T(256)S(1)} %get-tuple-element.39), channel_id=1, replica_groups=mesh['sect'=4,'ctx'=8,'tp'=8] {'tp'}, use_global_device_ids=true, to_apply=%region_4.5 | all-reduce | flops 256 | bytes 2048 | tf_op jit(solution)/shard_map/psum | solution.py:140
  137.2 5.1 %convolution_bitcast_fusion = f32[2048,256]{0,1:T(8,128)} fusion(bf16[2048,1024]{1,0:T(8,128)(2,1)} %param.22, bf16[256,1024]{1,0:T(8,128)(2,1)} %get-tuple-element.40, f32[1024]{0:T(1024)S(1)} %copy-done.6, f32[256]{0:T(256)S(1)} %add_rsqrt_fusion), kind=kOutput, calls=%fused_computation.18 | convolution fusion | flops 1074790400 | bytes 6820864 | tf_op jit(solution)/shard_map/dot_general | solution.py:145
  142.4 31.3 %reduce-scatter.2.cloned.1.call-done = f32[256,256]{0,1:T(8,128)} async-done(((f32[2048,256]{0,1:T(8,128)}), f32[256,256]{0,1:T(8,128)}) %reduce-scatter.2.cloned.1.call-update) | async-done | bytes 262160 | tf_op jit(solution)/shard_map/reduce_scatter | solution.py:144
  173.6 1.1 reshape.221
  174.7 0.1 slice.40
  174.9 0.1 slice.37
  175.0 0.7 copy.23
  175.7 0.6 fusion.96
  176.3 0.1 pad_maximum_fusion
  176.4 1.8 stack.2
  178.3 10.1 %all-to-all-start = ((bf16[32,1,128,256]{2,3,1,0:T(8,128)(2,1)}), bf16[32,1,128,256]{2,3,1,0:T(8,128)(2,1)}, u32[]{:S(2)}, u32[]{:S(2)}) async-start(bf16[32,1,128,256]{2,3,1,0:T(8,128)(2,1)} %stack.2), calls=%async_computation.1 | async-start | bytes 4194304 | tf_op jit(solution)/shard_map/all_to_all | solution.py:171
  188.4 79.1 %all-gather.6.cloned.1.call-done = bf16[1,1,128,8192]{3,2,1,0:T(8,128)(2,1)} async-done(((bf16[1,1,128,256]{3,2,1,0:T(8,128)(2,1)}), bf16[1,1,128,8192]{3,2,1,0:T(8,128)(2,1)}) %all-gather.6.cloned.1.call-update) | async-done | bytes 2097168 | tf_op jit(solution)/shard_map/all_gather | solution.py:176
  267.5 49.8 %conditional.1 = (f32[1,4,256]{2,1,0:T(4,128)S(1)}, f32[1,4,256,128]{3,2,1,0:T(8,128)S(1)}) conditional(s32[]{:T(128)} %convert_element_type.64, () %tuple.13, (s32[]{:T(128)}, s32[256]{0:T(256)S(1)}, s32[8192]{0:T(1024)S(1)}, bf16[1,128,32,256]{1,3,0,2:T(8,128)(2,1)}, bf16[256,512]{1,0:T(8,128)(2,1)S(1)}, ...), branch_computations={%region_6.7_spmd, %region_7.10_spmd} | conditional | flops 4389338112 | bytes 122481712 | solution.py:86
  267.5 3.7 %broadcast_compare_fusion = pred[256,8192]{0,1:T(8,128)(4,1)S(1)} fusion(s32[256]{0:T(256)S(1)} %broadcast_add_fusion, s32[8192]{0:T(1024)S(1)} %get-tuple-element.23), kind=kLoop, calls=%fused_computation.8 | loop fusion | flops 2097152 | bytes 2130944 | tf_op jit(solution)/shard_map/cond/branch_1_fun/ge | solution.py:50
  271.3 15.6 %fusion.2 = (f32[4,256]{1,0:T(4,128)S(1)}, f32[8192,256,4]{1,0,2:T(8,128)}) fusion(pred[256,8192]{0,1:T(8,128)(4,1)S(1)} %broadcast_compare_fusion, bf16[128,8192,1]{0,1,2:T(8,128)(2,1)} %bitcast.2, bf16[256,512]{1,0:T(8,128)(2,1)S(1)} %get-tuple-element.32), kind=kOutput, calls=%fused_computation.4 | convolution fusion | flops 2172648448 | bytes 38014976 | tf_op jit(solution)/shard_map/cond/branch_1_fun/rkgd,kdn->kgrn/dot_general | solution.py:47
  286.9 15.8 %fusion.8 = f32[1,4,256,128]{3,2,1,0:T(8,128)S(1)} fusion(bf16[1,128,8192]{2,1,0:T(8,128)(2,1)} %get-tuple-element.26, f32[8192,256,4]{1,0,2:T(8,128)} %get-tuple-element.42, f32[4,256]{1,0:T(4,128)S(1)} %broadcast_maximum_fusion, pred[256,8192]{0,1:T(8,128)(4,1)} %copy-done.1), kind=kOutput, calls=%fused_computation.10 | convolution fusion | flops 2181038080 | bytes 38277120 | tf_op jit(solution)/shard_map/cond/branch_1_fun/kgrn,kdn->kgrd/dot_general | solution.py:55
  302.7 14.6 %fusion.1 = f32[4,256]{1,0:T(4,128)S(1)} fusion(f32[8192,256,4]{1,0,2:T(8,128)} %get-tuple-element.42, f32[4,256]{1,0:T(4,128)S(1)} %broadcast_maximum_fusion, pred[256,8192]{0,1:T(8,128)(4,1)} %copy-done.1), kind=kLoop, calls=%fused_computation.3 | loop fusion | flops 33553408 | bytes 35659776 | tf_op jit(solution)/shard_map/cond/branch_1_fun/reduce_sum | solution.py:54
  317.3 0.2 fusion.56
  317.5 0.2 copy.21
  317.7 0.7 copy.33
  (31 shorter events, 0.2 us)
Async XLA Ops:
  6.5 76.3 %copy-start = (bf16[1280,1024]{1,0:T(8,128)(2,1)S(1)}, bf16[1280,1024]{1,0:T(8,128)(2,1)}, u32[]{:S(2)}) copy-start(bf16[1280,1024]{1,0:T(8,128)(2,1)} %param.18) | copy-start | bytes 7864324
  6.5 76.3 %all-reduce.2.cloned.1.call-start = ((), (), s32[]{:S(2)}) async-start(), calls=%async_computation.2 | async-start | bytes 1310720 | tf_op jit(solution)/shard_map/psum | solution.py:123
  9.0 73.8 %copy-start.2 = (bf16[128,1280]{1,0:T(8,128)(2,1)S(1)}, bf16[128,1280]{1,0:T(8,128)(2,1)}, u32[]{:S(2)}) copy-start(bf16[128,1280]{1,0:T(8,128)(2,1)} %param.13) | copy-start | bytes 983044
  13.4 71.8 %copy-start.4 = (s32[2]{0:T(128)S(1)}, s32[2]{0:T(128)}, u32[]{:S(2)}) copy-start(s32[2]{0:T(128)} %param.20) | copy-start | bytes 28
  13.4 107.8 %copy-start.3 = (bf16[256,1024]{1,0:T(8,128)(2,1)S(1)}, bf16[256,1024]{1,0:T(8,128)(2,1)}, u32[]{:S(2)}) copy-start(bf16[256,1024]{1,0:T(8,128)(2,1)} %param.19) | copy-start | bytes 1572868
  13.5 123.7 %copy-start.6 = (f32[1024]{0:T(1024)S(1)}, f32[1024]{0:T(1024)}, u32[]{:S(2)}) copy-start(f32[1024]{0:T(1024)} %param.21) | copy-start | bytes 12292
  13.5 106.5 %all-gather.4.cloned.1.call-start = ((), (), s32[]{:S(2)}) async-start(), calls=%async_computation.3 | async-start | bytes 1310720 | tf_op jit(solution)/shard_map/all_gather | solution.py:131
  85.2 88.5 %reduce-scatter.2.cloned.1.call-start = ((), (), s32[]{:S(2)}) async-start(), calls=%async_computation.4 | async-start | bytes 2359296 | tf_op jit(solution)/shard_map/reduce_scatter | solution.py:144
  142.3 125.2 %copy-start.5 = (bf16[256,512]{1,0:T(8,128)(2,1)S(1)}, bf16[256,512]{1,0:T(8,128)(2,1)}, u32[]{:S(2)}) copy-start(bf16[256,512]{1,0:T(8,128)(2,1)} %param.23) | copy-start | bytes 786436
  142.3 125.2 %all-gather.6.cloned.1.call-start = ((), (), s32[]{:S(2)}) async-start(), calls=%async_computation.5 | async-start | bytes 2162688 | tf_op jit(solution)/shard_map/all_gather | solution.py:176
  178.3 89.2 %all-to-all-start = ((bf16[32,1,128,256]{2,3,1,0:T(8,128)(2,1)}), bf16[32,1,128,256]{2,3,1,0:T(8,128)(2,1)}, u32[]{:S(2)}, u32[]{:S(2)}) async-start(bf16[32,1,128,256]{2,3,1,0:T(8,128)(2,1)} %stack.2), calls=%async_computation.1 | async-start | bytes 4194304 | tf_op jit(solution)/shard_map/all_to_all | solution.py:171
  271.3 15.6 %copy-start.1 = (pred[256,8192]{0,1:T(8,128)(4,1)}, pred[256,8192]{0,1:T(8,128)(4,1)S(1)}, u32[]{:S(2)}) copy-start(pred[256,8192]{0,1:T(8,128)(4,1)S(1)} %broadcast_compare_fusion) | copy-start | bytes 6291460 | tf_op jit(solution)/shard_map/cond
Sparse Core Ops, SparseCore 0:
  13.6 69.2 all-reduce.1
  85.3 34.6 all-gather.3
  142.4 31.1 reduce-scatter.1
  176.0 91.4 all-gather.5
